TPU v7x, 256 devices: a whole 4x4x8 slice. The times are simulated.
256 devices in a mesh: lon: 32 (over z_lo, x, core), lat: 8 (over y, z_hi).
Axes of the slice: x: 4, y: 4, z: 8 (z_hi: 2, z_lo: 4; z = z_hi * 4 + z_lo), core: 2. Of those that a mesh axis runs over, the one named last changes fastest.
Arguments:
- tracers: float32 [6, 128, 64, 4096], P(None, None, 'lat', 'lon'), may hold values from 0.2 to 5
- courant_x: float32 [128, 64, 4096], P(None, 'lat', 'lon'), may hold values from -0.24 to 0.24
- courant_y: float32 [128, 64, 4096], P(None, 'lat', 'lon'), may hold values from -0.24 to 0.24
- sunlit: int32 [64, 4096], P('lat', 'lon'), may hold values from 0 to 1, as said below
- cosine_zenith: float32 [64, 4096], P('lat', 'lon'), may hold values from 0.1 to 1
- albedo: float32 [64, 4096], P('lat', 'lon'), may hold values from 0.05 to 0.7
- absorb: float32 [8, 6], replicated, may hold values from 0.0002 to 0.01
- scatter: float32 [8], replicated, may hold values from 0.001 to 0.05
- solar_weight: float32 [8], replicated, may hold values from 0.2 to 2
Outputs:
- tracers_next: float32 [6, 128, 64, 4096], P(None, None, 'lat', 'lon')
- heating: float32 [128, 64, 4096], P(None, 'lat', 'lon')
Inputs may be any that keep to these rules, and one draw needn't show every extreme that they name: Of two columns in one latitude row 2048 longitudes apart, exactly one is sunlit; in each row the sunlit columns form one run of 2048 longitudes around the cycle.
All inputs are finite; a program needn't handle non-finite values.
Results may differ from a plain program's by a relative error of at most 0.00005.
Values sent between devices are 32-bit elements; how exact they have to be, the bound alone decides.
A program may use at most 128 MiB of HBM per device.

v0:
```python
import jax
import jax.numpy as jnp
from jax import lax
from jax.experimental import pallas as pl
from jax.experimental.pallas import tpu as pltpu
from jax.sharding import PartitionSpec as P

MESH = pl.DeviceIdType.MESH
LOG2E = 1.4426950408889634
CHUNK = 16
AHEAD = 2
SHARED = 3
CY, NA, NB, SA, SB, RELAY = range(6)


def rcp(value):
    return pltpu.reciprocal(value, approx=True)


def sweep(beams, keep, nn):
    kp, kq, kd, ka, ks = keep
    levels = nn.shape[0]

    def step(level, state):
        state_new = []
        for i, (dn, beam, net) in enumerate(state):
            at = pl.ds(8 * i, 8)
            dn = kp[level, at, :] * dn + kq[level, at, :] * beam
            beam = beam * kd[level, at, :]
            below = dn * ka[level, at, :] + beam * ks[level, at, :]
            nn[level, at, :] = net - below
            state_new.append((dn, beam, below))
        return tuple(state_new)

    state = tuple((jnp.zeros_like(beam), beam, net) for beam, net in beams)
    lax.fori_loop(0, levels, step, state, unroll=8)


def summed(nn, group, i):
    levels, depth, lanes = nn.shape
    flat = nn.reshape(levels * depth, lanes)
    parts = [flat[pl.ds(group * 8 * depth + 8 * i + g, 8, stride=depth), :] for g in range(8)]
    while len(parts) > 1:
        parts = [a + b for a, b in zip(parts[::2], parts[1::2], strict=True)]
    return parts[0]


def finish(tn, heat, op, oq, od, oa, os, start_state, tn_out, heat_out, nn, full, sem):
    levels = nn.shape[0]
    rows = heat.shape[0] // levels
    moved = pltpu.make_async_copy(tn, tn_out, sem.at[0])
    moved.start()
    beams = [
        (start_state[pl.ds(16 * i, 8), :], start_state[pl.ds(16 * i + 8, 8), :]) for i in range(2)
    ]
    sweep(beams, (op, oq, od, oa, os), nn)

    def total(group, carry):
        at = pl.ds(pl.multiple_of(group * 8 * rows, 8 * rows), 8 * rows)
        full[at, :] = heat[at, :]
        for i, r in enumerate((0, rows - 1)):
            full[pl.ds(group * 8 * rows + r, 8, stride=rows), :] = summed(nn, group, i)
        return carry

    lax.fori_loop(0, levels // 8, total, 0, unroll=2)
    heated = pltpu.make_async_copy(full, heat_out, sem.at[1])
    heated.start()
    moved.wait()
    heated.wait()


def kernel(
    x4, x3, cx3, cy4, cy3, sunlit_in, cosine_in, albedo_in, absorb_in, scatter_in, weight_in,
    tn, heat, op, oq, od, oa, os, start_state,
    x, cx, cy, sunlit, cosine, albedo, absorb, scatter, weight,
    north, south, relay, pack_e, pack_w, from_e, from_w,
    cp, cq, cd, ca, cs, nn,
    load_sem, send_sem, recv_sem, lon_send, lon_recv, hop_send,
):
    tracers, levels = x4.shape[0], x4.shape[1]
    rows, lanes = x4.shape[2], x4.shape[3]
    chunks = levels // CHUNK
    lon, lat = lax.axis_index("lon"), lax.axis_index("lat")
    n_lon, n_lat = lax.axis_size("lon"), lax.axis_size("lat")
    has_n, has_s = lat < n_lat - 1, lat > 0
    to_n, to_s = (lon, lat + 1), (lon, lat - 1)
    to_e, to_w = (lax.rem(lon + 1, n_lon), lat), (lax.rem(lon + n_lon - 1, n_lon), lat)
    first, last = lat == 0, lat == n_lat - 1
    via_s, via_n = lat == 2, lat == n_lat - 3
    lo, hi = pl.ds(0, SHARED), pl.ds(SHARED, tracers - SHARED)

    pairs = (
        (x3, x), (cx3, cx), (cy3, cy), (sunlit_in, sunlit), (cosine_in, cosine),
        (albedo_in, albedo), (absorb_in, absorb), (scatter_in, scatter), (weight_in, weight),
    )
    loads = [pltpu.make_async_copy(a, b, load_sem.at[i]) for i, (a, b) in enumerate(pairs)]
    for c in loads:
        c.start()

    barrier = pltpu.get_barrier_semaphore()
    partners = [
        (None, to_e),
        (None, to_w),
        (has_n, to_n),
        (has_s, to_s),
        (first, (lon, lat + 2)),
        (via_s, (lon, lat - 2)),
        (last, (lon, lat - 2)),
        (via_n, (lon, lat + 2)),
    ]
    for here, device in partners:
        if here is None:
            pl.semaphore_signal(barrier, inc=1, device_id=device, device_id_type=MESH)
        else:

            @pl.when(here)
            def _():
                pl.semaphore_signal(barrier, inc=1, device_id=device, device_id_type=MESH)

    peers = 2
    for here, _ in partners[2:]:
        peers = peers + here.astype(jnp.int32)
    pl.semaphore_wait(barrier, peers)

    def copy(src, dst, k, kind, device):
        return pltpu.make_async_remote_copy(
            src_ref=src,
            dst_ref=dst,
            send_sem=send_sem.at[k, kind],
            recv_sem=recv_sem.at[k, kind],
            device_id=device,
            device_id_type=MESH,
        )

    def part(k):
        return pl.ds(levels - (k + 1) * CHUNK, CHUNK)

    def send_cy(k):
        return copy(cy4.at[part(k), rows - 1, :], south.at[tracers, part(k)], k, CY, to_n)

    def send_na(k):
        return copy(x4.at[lo, part(k), rows - 1, :], south.at[lo, part(k)], k, NA, to_n)

    def send_nb(k):
        return copy(x4.at[hi, part(k), rows - 1, :], south.at[hi, part(k)], k, NB, to_n)

    def send_sa(k):
        return copy(x4.at[lo, part(k), 0, :], north.at[lo, part(k)], k, SA, to_s)

    def send_sb(k):
        return copy(x4.at[hi, part(k), 0, :], north.at[hi, part(k)], k, SB, to_s)

    def send_rs(k):
        return copy(x4.at[hi, part(k), 0, :], relay.at[:, part(k)], k, RELAY, (lon, lat - 2))

    def send_rn(k):
        return copy(x4.at[hi, part(k), rows - 1, :], relay.at[:, part(k)], k, RELAY, (lon, lat + 2))

    def hop(k, dst, kind, device):
        return pltpu.make_async_remote_copy(
            src_ref=relay.at[:, part(k)],
            dst_ref=dst.at[hi, part(k)],
            send_sem=hop_send.at[k],
            recv_sem=recv_sem.at[k, kind],
            device_id=device,
            device_id_type=MESH,
        )

    direct_nb = jnp.logical_and(has_n, jnp.logical_not(via_n))
    direct_sb = jnp.logical_and(has_s, jnp.logical_not(via_s))
    detour = [(via_s, send_rs), (via_n, send_rn)]
    outgoing = [
        (has_n, send_cy),
        (has_n, send_na),
        (has_s, send_sa),
        (direct_nb, send_nb),
        (direct_sb, send_sb),
    ]

    def pass_on(k):
        @pl.when(first)
        def _():
            send_rs(k).wait_recv()
            hop(k, north, SB, to_n).start()

        @pl.when(last)
        def _():
            send_rn(k).wait_recv()
            hop(k, south, NB, to_s).start()

    def send(k, which):
        for here, make in which:

            @pl.when(here)
            def _():
                make(k).start()

    for k in range(chunks):
        send(k, detour)
    for k in range(AHEAD):
        send(k, outgoing)

    @pl.when(last)
    def _():
        north[...] = jnp.zeros_like(north)

    @pl.when(first)
    def _():
        south[...] = jnp.zeros_like(south)

    for c in loads:
        c.wait()

    lane = lax.broadcasted_iota(jnp.int32, (rows, lanes), 1)
    sub = lax.broadcasted_iota(jnp.int32, (rows, lanes), 0)

    def tile(level):
        return pl.ds(pl.multiple_of(level * rows, rows), rows)

    def pack(level, packed):
        shift = lax.rem(level + 1, lanes)
        west, east, flow = packed
        at_e, at_w = lane == level, lane == shift
        west_new, east_new = [], []
        for t in range(tracers):
            turned = pltpu.roll(x[t, tile(level), :], shift, 1)
            west_new.append(jnp.where(at_w, turned, west[t]))
            east_new.append(jnp.where(at_e, turned, east[t]))
        flow = jnp.where(at_e, pltpu.roll(cx[tile(level), :], shift, 1), flow)
        return tuple(west_new), tuple(east_new), flow

    zero = jnp.zeros((rows, lanes), jnp.float32)
    west, east, flow = lax.fori_loop(
        0, levels, pack, ((zero,) * tracers, (zero,) * tracers, zero), unroll=16
    )
    for t in range(tracers):
        pack_w[t] = west[t]
        pack_e[t] = east[t]
    pack_e[tracers] = flow
    go_w = pltpu.make_async_remote_copy(
        src_ref=pack_w, dst_ref=from_e, send_sem=lon_send.at[0], recv_sem=lon_recv.at[0],
        device_id=to_w, device_id_type=MESH,
    )
    go_e = pltpu.make_async_remote_copy(
        src_ref=pack_e, dst_ref=from_w, send_sem=lon_send.at[1], recv_sem=lon_recv.at[1],
        device_id=to_e, device_id_type=MESH,
    )
    go_w.start()
    go_e.start()
    for k in range(AHEAD):
        pass_on(k)
    go_w.wait()
    go_e.wait()
    for k in range(AHEAD, chunks):
        pass_on(k)
        send(k, outgoing)
    flow = from_w[tracers]
    for t in range(tracers):
        own = pltpu.roll(pack_w[t], lanes - 1, 1)
        from_w[t] = jnp.maximum(flow, 0.0) * from_w[t] + jnp.minimum(flow, 0.0) * own

    def advect(level, carry):
        to_first = lax.rem(2 * lanes - level, lanes)
        to_last = lax.rem(2 * lanes - 2 - level, lanes)
        here_x = cx[tile(level), :]
        here_y = jnp.where(sub == rows - 1, 0.0, cy[tile(level), :])
        xp, xm = jnp.maximum(here_x, 0.0), jnp.minimum(here_x, 0.0)
        yp, ym = jnp.maximum(here_y, 0.0), jnp.minimum(here_y, 0.0)
        for t in range(tracers):
            q = x[t, tile(level), :]
            ahead = jnp.where(
                lane == lanes - 1, pltpu.roll(from_e[t], to_last, 1), pltpu.roll(q, lanes - 1, 1)
            )
            flux_e = xp * q + xm * ahead
            flux_w = jnp.where(
                lane == 0, pltpu.roll(from_w[t], to_first, 1), pltpu.roll(flux_e, 1, 1)
            )
            flux_n = yp * q + ym * pltpu.roll(q, rows - 1, 0)
            flux_s = pltpu.roll(flux_n, 1, 0)
            tn[t, tile(level), :] = q - (flux_e - flux_w) - (flux_n - flux_s)
        return carry

    gs = absorb.shape[0]
    fold = -2.0 * LOG2E
    scat, wgt = zero, zero
    for g in range(gs):
        scat = jnp.where(sub == g, scatter[g], scat)
        wgt = jnp.where(sub == g, weight[g], wgt)
    coef = [jnp.broadcast_to(absorb[:, t : t + 1], (gs, lanes)) for t in range(tracers)]
    coef[0] = coef[0] + scat
    coef = [c * fold for c in coef]
    scat = scat * (0.9 * fold)

    def spread(ref, row):
        return jnp.broadcast_to(ref[row : row + 1, :], (gs, lanes))

    def up(which, keep, level, carry):
        half_inv = [0.5 / spread(cosine, r) for r in which]
        carry_new = []
        kp, kq, kd, ka, ks = keep
        for i, (r, half, (a, s)) in enumerate(zip(which, half_inv, carry, strict=True)):
            q = [
                jnp.broadcast_to(tn[t, pl.ds(level * rows + r, 1), :], (gs, lanes))
                for t in range(tracers)
            ]
            opt = coef[0] * q[0]
            for t in range(1, tracers):
                opt = opt + coef[t] * q[t]
            single = scat * q[0] * rcp(opt)
            square = (1.0 - single) * (1.0 - 0.85 * single)
            h = square * lax.rsqrt(square)
            e = jnp.exp2(h * opt)
            direct = jnp.exp2(opt * half)
            e2 = e * e
            u = 1.0 - e2
            inv = rcp(h * (1.0 + e2) + (1.0 - 0.925 * single) * u)
            back = 0.075 * single
            refl = back * (u * inv)
            trans = (e + e) * (h * inv)
            refl_dir = back * (1.0 - direct)
            trans_dir = (0.925 / 0.075) * refl_dir
            d = rcp(1.0 - refl * a)
            p = trans * d
            sd = s * direct
            at = pl.ds(i * gs, gs)
            kp[level, at, :] = p
            kq[level, at, :] = (refl * sd + trans_dir) * d
            kd[level, at, :] = direct
            ka[level, at, :] = 1.0 - a
            ks[level, at, :] = 1.0 - s
            a_new = refl + (trans * a) * p
            s_new = refl_dir + p * (sd + a * trans_dir)
            carry_new.append((a_new, s_new))
        return tuple(carry_new)

    def ground(which):
        return tuple((spread(albedo, r), spread(albedo, r)) for r in which)

    def top(which, carry):
        beams = []
        for r, (_, s) in zip(which, carry, strict=True):
            lit = spread(sunlit, r).astype(jnp.float32)
            beam = (4.0 * lit) * wgt * spread(cosine, r)
            beams.append((beam, beam * (1.0 - s)))
        return beams

    inner = tuple(range(1, rows - 1))
    lax.fori_loop(0, levels, advect, 0, unroll=4)
    carry = ground(inner)
    for k in range(chunks):
        start = levels - 1 - k * CHUNK
        carry = lax.fori_loop(
            0, CHUNK, lambda i, c: up(inner, (cp, cq, cd, ca, cs), start - i, c), carry, unroll=4
        )
    sweep(top(inner, carry), (cp, cq, cd, ca, cs), nn)

    def total(group, carry):
        for i, r in enumerate(inner):
            heat[pl.ds(group * 8 * rows + r, 8, stride=rows), :] = summed(nn, group, i)
        return carry

    lax.fori_loop(0, levels // 8, total, 0)

    outer = (0, rows - 1)
    carry = ground(outer)

    def every(level, row):
        return pl.ds(level * rows + row, 8, stride=rows)

    for k in range(chunks):
        for here, make in (
            (has_s, send_cy), (has_s, send_na), (has_s, send_nb), (has_n, send_sa), (has_n, send_sb),
        ):

            @pl.when(here)
            def _():
                make(k).wait_recv()

        for level in range(levels - (k + 1) * CHUNK, levels - k * CHUNK, 8):
            group = pl.ds(level, 8)
            flow_n = jnp.where(last, 0.0, cy[every(level, rows - 1), :])
            flow_s = south[tracers, group, :]
            np_, nm = jnp.maximum(flow_n, 0.0), jnp.minimum(flow_n, 0.0)
            sp, sm = jnp.maximum(flow_s, 0.0), jnp.minimum(flow_s, 0.0)
            for t in range(tracers):
                flux_n = np_ * x[t, every(level, rows - 1), :] + nm * north[t, group, :]
                flux_s = sp * south[t, group, :] + sm * x[t, every(level, 0), :]
                at_n, at_s = every(level, rows - 1), every(level, 0)
                tn[t, at_n, :] = tn[t, at_n, :] - flux_n
                tn[t, at_s, :] = tn[t, at_s, :] + flux_s
        start = levels - 1 - k * CHUNK
        carry = lax.fori_loop(
            0, CHUNK, lambda i, c: up(outer, (op, oq, od, oa, os), start - i, c), carry, unroll=4
        )
    for i, (beam, net) in enumerate(top(outer, carry)):
        start_state[pl.ds(2 * i * gs, gs), :] = beam
        start_state[pl.ds((2 * i + 1) * gs, gs), :] = net

    for k in range(chunks):
        for here, make in outgoing + detour:

            @pl.when(here)
            def _():
                make(k).wait_send()

        @pl.when(first)
        def _():
            hop(k, north, SB, to_n).wait_send()

        @pl.when(last)
        def _():
            hop(k, south, NB, to_s).wait_send()


def on_device(tracers, courant_x, courant_y, sunlit, cosine, albedo, absorb, scatter, weight):
    count, levels, rows, lanes = tracers.shape
    gs = absorb.shape[0]
    chunks = levels // CHUNK
    f32 = jnp.float32
    hbm = pl.BlockSpec(memory_space=pltpu.HBM)
    vmem = pl.BlockSpec(memory_space=pltpu.VMEM)
    dma = pltpu.SemaphoreType.DMA
    flat = levels * rows
    inner_layers = pltpu.VMEM((levels, (rows - 2) * gs, lanes), f32)
    outer_layers = pltpu.VMEM((levels, 2 * gs, lanes), f32)
    operands = (
        tracers,
        tracers.reshape(count, flat, lanes),
        courant_x.reshape(flat, lanes),
        courant_y,
        courant_y.reshape(flat, lanes),
        sunlit,
        cosine,
        albedo,
        absorb,
        scatter,
        weight,
    )
    held = pl.pallas_call(
        kernel,
        out_shape=[pltpu.VMEM((count, flat, lanes), f32), pltpu.VMEM((flat, lanes), f32)]
        + [outer_layers] * 5
        + [pltpu.VMEM((4 * gs, lanes), f32)],
        in_specs=[hbm] * 11,
        out_specs=[vmem] * 8,
        scratch_shapes=[
            pltpu.VMEM((count, flat, lanes), f32),
            pltpu.VMEM((flat, lanes), f32),
            pltpu.VMEM((flat, lanes), f32),
            pltpu.VMEM((rows, lanes), jnp.int32),
            pltpu.VMEM((rows, lanes), f32),
            pltpu.VMEM((rows, lanes), f32),
            pltpu.VMEM(absorb.shape, f32),
            pltpu.SMEM((gs,), f32),
            pltpu.SMEM((gs,), f32),
            pltpu.VMEM((count, levels, lanes), f32),
            pltpu.VMEM((count + 1, levels, lanes), f32),
            pltpu.VMEM((count - SHARED, levels, lanes), f32),
            pltpu.VMEM((count + 1, rows, lanes), f32),
            pltpu.VMEM((count, rows, lanes), f32),
            pltpu.VMEM((count, rows, lanes), f32),
            pltpu.VMEM((count + 1, rows, lanes), f32),
        ]
        + [inner_layers] * 6
        + [dma((9,)), dma((chunks, 6)), dma((chunks, 6)), dma((2,)), dma((2,)), dma((chunks,))],
        compiler_params=pltpu.CompilerParams(
            collective_id=0, has_side_effects=True, vmem_limit_bytes=36 * 2**20
        ),
        name="advect_and_heat",
    )(*[pltpu.with_memory_space_constraint(a, pltpu.HBM) for a in operands])
    moved, heating = pl.pallas_call(
        finish,
        out_shape=[pltpu.HBM((count, flat, lanes), f32), pltpu.HBM((flat, lanes), f32)],
        in_specs=[vmem] * 8,
        out_specs=[hbm] * 2,
        scratch_shapes=[outer_layers, pltpu.VMEM((flat, lanes), f32), dma((2,))],
        compiler_params=pltpu.CompilerParams(vmem_limit_bytes=8 * 2**20),
        name="finish",
    )(*[pltpu.with_memory_space_constraint(a, pltpu.VMEM) for a in held])
    return moved.reshape(tracers.shape), heating.reshape(levels, rows, lanes)


def solution(mesh):
    in_specs = (
        P(None, None, "lat", "lon"),
        P(None, "lat", "lon"),
        P(None, "lat", "lon"),
        P("lat", "lon"),
        P("lat", "lon"),
        P("lat", "lon"),
        P(),
        P(),
        P(),
    )
    out_specs = (P(None, None, "lat", "lon"), P(None, "lat", "lon"))
    return jax.shard_map(
        on_device, mesh=mesh, in_specs=in_specs, out_specs=out_specs, check_vma=False
    )
```

profile of v0, /device:TPU:40, one launch (start us, length us, event | category | flops | bytes accessed | tf_op | source)
XLA Modules:
  0.0 49.9 jit_solution(5637671941857612792)
XLA Ops:
  0.6 47.5 %advect_and_heat.1 = (f32[6,1024,128]{2,1,0:T(8,128)S(1)}, f32[1024,128]{1,0:T(8,128)S(1)}, f32[128,16,128]{2,1,0:T(8,128)S(1)}, f32[128,16,128]{2,1,0:T(8,128)S...) custom-call(f32[6,128,8,128]{3,2,1,0:T(8,128)} %x4.1, ...), custom_call_target="tpu_custom_call" | custom-call | tf_op jit(solution)/shard_map/advect_and_heat/pallas_call | solution.py:439
  48.1 1.8 %finish.1 = (f32[6,1024,128]{2,1,0:T(8,128)}, f32[1024,128]{1,0:T(8,128)}) custom-call(f32[6,1024,128]{2,1,0:T(8,128)S(1)} %get-tuple-element.12.tn, f32[1024,128]{1,0:T(8,128)S(1)} %get-tuple-element.13.heat, f32[128,16,128]{2,1,0:T(8,128)S(1)} %get-tuple-element.14.op, f32[128,16,128]{2,1,0:T(8,128)S(1)} %get-tuple-element.15.oq, ...), custom_call_target="tpu_custom_call" | custom-call | tf_op jit(solution)/shard_map/finish/pallas_call | solution.py:471
where the time goes:
time: 50 us; the launch traced here: 49.9 us
  Pallas kernels  49.3 us (99%)
  between operations  0.64 us (1%)
    pallas_call x1, Pallas kernels, on_device(): pl.pallas_call(kernel, out_shape=[pltpu.VMEM((count, flat, lanes), f32),...  47.5 us
    pallas_call x1, Pallas kernels, on_device(): pl.pallas_call(finish, out_shape=[pltpu.HBM((count, flat, lanes), f32), p...  1.85 us

commit v1 on v0

--- a/solution.py
+++ b/solution.py
@@ -1,3 +1,5 @@
+import functools
+
 import jax
 import jax.numpy as jnp
 from jax import lax
@@ -7,9 +9,7 @@
 
 MESH = pl.DeviceIdType.MESH
 LOG2E = 1.4426950408889634
-CHUNK = 16
-AHEAD = 2
-SHARED = 3
+PARTS = ((96, 32), (48, 48), (16, 32), (0, 16))
 CY, NA, NB, SA, SB, RELAY = range(6)
 
 
@@ -75,23 +75,34 @@
     x, cx, cy, sunlit, cosine, albedo, absorb, scatter, weight,
     north, south, relay, pack_e, pack_w, from_e, from_w,
     cp, cq, cd, ca, cs, nn,
-    load_sem, send_sem, recv_sem, lon_send, lon_recv, hop_send,
+    load_sem, send_sem, recv_sem, lon_send, lon_recv, relay_recv, hop_send,
 ):
     tracers, levels = x4.shape[0], x4.shape[1]
     rows, lanes = x4.shape[2], x4.shape[3]
-    chunks = levels // CHUNK
+    chunks = len(PARTS)
     lon, lat = lax.axis_index("lon"), lax.axis_index("lat")
     n_lon, n_lat = lax.axis_size("lon"), lax.axis_size("lat")
     has_n, has_s = lat < n_lat - 1, lat > 0
     to_n, to_s = (lon, lat + 1), (lon, lat - 1)
     to_e, to_w = (lax.rem(lon + 1, n_lon), lat), (lax.rem(lon + n_lon - 1, n_lon), lat)
     first, last = lat == 0, lat == n_lat - 1
-    via_s, via_n = lat == 2, lat == n_lat - 3
-    lo, hi = pl.ds(0, SHARED), pl.ds(SHARED, tracers - SHARED)
+    middle = jnp.logical_and(has_n, has_s)
+    even = lax.rem(lat, 2) == 0
+    via_first = jnp.logical_and(middle, even)
+    via_last = jnp.logical_and(middle, jnp.logical_not(even))
+    slots = relay.shape[0]
+    slot = lax.div(lat - 1, 2)
+
+    def direct(k):
+        return pl.ds(0, tracers - 1 - k % 2)
+
+    def shared(k):
+        return pl.ds(tracers - 1 - k % 2, 1 + k % 2)
 
     pairs = (
-        (x3, x), (cx3, cx), (cy3, cy), (sunlit_in, sunlit), (cosine_in, cosine),
-        (albedo_in, albedo), (absorb_in, absorb), (scatter_in, scatter), (weight_in, weight),
+        (cx3, cx), *[(x3.at[t], x.at[t]) for t in range(tracers)],
+        (cy3, cy), (sunlit_in, sunlit), (cosine_in, cosine), (albedo_in, albedo),
+        (absorb_in, absorb), (scatter_in, scatter), (weight_in, weight),
     )
     loads = [pltpu.make_async_copy(a, b, load_sem.at[i]) for i, (a, b) in enumerate(pairs)]
     for c in loads:
@@ -103,11 +114,14 @@
         (None, to_w),
         (has_n, to_n),
         (has_s, to_s),
-        (first, (lon, lat + 2)),
-        (via_s, (lon, lat - 2)),
-        (last, (lon, lat - 2)),
-        (via_n, (lon, lat + 2)),
+        (jnp.logical_and(middle, lat > 1), (lon, 0)),
+        (jnp.logical_and(middle, lat < n_lat - 2), (lon, n_lat - 1)),
     ]
+    for other in range(1, n_lat - 1):
+        if other > 1:
+            partners.append((first, (lon, other)))
+        if other < n_lat - 2:
+            partners.append((last, (lon, other)))
     for here, device in partners:
         if here is None:
             pl.semaphore_signal(barrier, inc=1, device_id=device, device_id_type=MESH)
@@ -120,8 +134,6 @@
     peers = 2
     for here, _ in partners[2:]:
         peers = peers + here.astype(jnp.int32)
-    pl.semaphore_wait(barrier, peers)
-
     def copy(src, dst, k, kind, device):
         return pltpu.make_async_remote_copy(
             src_ref=src,
@@ -133,60 +145,101 @@
         )
 
     def part(k):
-        return pl.ds(levels - (k + 1) * CHUNK, CHUNK)
+        return pl.ds(*PARTS[k])
 
     def send_cy(k):
         return copy(cy4.at[part(k), rows - 1, :], south.at[tracers, part(k)], k, CY, to_n)
 
+    def rows_to_n(k, planes, kind):
+        src, dst = x4.at[planes, part(k), rows - 1, :], south.at[planes, part(k)]
+        return copy(src, dst, k, kind, to_n)
+
+    def rows_to_s(k, planes, kind):
+        src, dst = x4.at[planes, part(k), 0, :], north.at[planes, part(k)]
+        return copy(src, dst, k, kind, to_s)
+
     def send_na(k):
-        return copy(x4.at[lo, part(k), rows - 1, :], south.at[lo, part(k)], k, NA, to_n)
+        return rows_to_n(k, direct(k), NA)
 
     def send_nb(k):
-        return copy(x4.at[hi, part(k), rows - 1, :], south.at[hi, part(k)], k, NB, to_n)
+        return rows_to_n(k, shared(k), NB)
+
+    def send_n(k):
+        return rows_to_n(k, pl.ds(0, tracers), NA)
 
     def send_sa(k):
-        return copy(x4.at[lo, part(k), 0, :], north.at[lo, part(k)], k, SA, to_s)
+        return rows_to_s(k, direct(k), SA)
 
     def send_sb(k):
-        return copy(x4.at[hi, part(k), 0, :], north.at[hi, part(k)], k, SB, to_s)
-
-    def send_rs(k):
-        return copy(x4.at[hi, part(k), 0, :], relay.at[:, part(k)], k, RELAY, (lon, lat - 2))
-
-    def send_rn(k):
-        return copy(x4.at[hi, part(k), rows - 1, :], relay.at[:, part(k)], k, RELAY, (lon, lat + 2))
-
-    def hop(k, dst, kind, device):
+        return rows_to_s(k, shared(k), SB)
+
+    def send_s(k):
+        return rows_to_s(k, pl.ds(0, tracers), SA)
+
+    def detour_row(k, row, at, to):
         return pltpu.make_async_remote_copy(
-            src_ref=relay.at[:, part(k)],
-            dst_ref=dst.at[hi, part(k)],
-            send_sem=hop_send.at[k],
-            recv_sem=recv_sem.at[k, kind],
-            device_id=device,
+            src_ref=x4.at[shared(k), part(k), row, :],
+            dst_ref=relay.at[at, pl.ds(0, 1 + k % 2), part(k)],
+            send_sem=send_sem.at[k, RELAY],
+            recv_sem=relay_recv.at[k, at],
+            device_id=(lon, to),
             device_id_type=MESH,
         )
 
-    direct_nb = jnp.logical_and(has_n, jnp.logical_not(via_n))
-    direct_sb = jnp.logical_and(has_s, jnp.logical_not(via_s))
-    detour = [(via_s, send_rs), (via_n, send_rn)]
+    def send_rs(k):
+        return detour_row(k, 0, slot, 0)
+
+    def send_rn(k):
+        return detour_row(k, rows - 1, slot, n_lat - 1)
+
+    def hop(k, at, dst, kind, to):
+        return pltpu.make_async_remote_copy(
+            src_ref=relay.at[at, pl.ds(0, 1 + k % 2), part(k)],
+            dst_ref=dst.at[shared(k), part(k)],
+            send_sem=hop_send.at[k, at],
+            recv_sem=recv_sem.at[k, kind],
+            device_id=(lon, to),
+            device_id_type=MESH,
+        )
+
+    def hop_s(k, at):
+        return hop(k, at, north, SB, 2 * at + 1)
+
+    def hop_n(k, at):
+        return hop(k, at, south, NB, 2 * at + 2)
+
+    detour = [(via_first, send_rs), (via_last, send_rn)]
     outgoing = [
         (has_n, send_cy),
-        (has_n, send_na),
-        (has_s, send_sa),
-        (direct_nb, send_nb),
-        (direct_sb, send_sb),
+        (jnp.logical_and(has_n, jnp.logical_not(via_last)), send_n),
+        (via_last, send_na),
+        (jnp.logical_and(has_s, jnp.logical_not(via_first)), send_s),
+        (via_first, send_sa),
     ]
+    whole_s, split_s = jnp.logical_and(has_s, jnp.logical_not(even)), jnp.logical_and(has_s, even)
+    whole_n, split_n = jnp.logical_and(has_n, even), jnp.logical_and(has_n, jnp.logical_not(even))
+    incoming = [
+        (has_s, send_cy),
+        (whole_s, send_n),
+        (split_s, send_na),
+        (split_s, send_nb),
+        (whole_n, send_s),
+        (split_n, send_sa),
+        (split_n, send_sb),
+    ]
 
     def pass_on(k):
-        @pl.when(first)
-        def _():
-            send_rs(k).wait_recv()
-            hop(k, north, SB, to_n).start()
-
-        @pl.when(last)
-        def _():
-            send_rn(k).wait_recv()
-            hop(k, south, NB, to_s).start()
+        for at in range(slots):
+
+            @pl.when(first)
+            def _():
+                detour_row(k, 0, at, 0).wait_recv()
+                hop_s(k, at).start()
+
+            @pl.when(last)
+            def _():
+                detour_row(k, rows - 1, at, n_lat - 1).wait_recv()
+                hop_n(k, at).start()
 
     def send(k, which):
         for here, make in which:
@@ -194,11 +247,6 @@
             @pl.when(here)
             def _():
                 make(k).start()
-
-    for k in range(chunks):
-        send(k, detour)
-    for k in range(AHEAD):
-        send(k, outgoing)
 
     @pl.when(last)
     def _():
@@ -208,35 +256,39 @@
     def _():
         south[...] = jnp.zeros_like(south)
 
-    for c in loads:
-        c.wait()
-
     lane = lax.broadcasted_iota(jnp.int32, (rows, lanes), 1)
     sub = lax.broadcasted_iota(jnp.int32, (rows, lanes), 0)
 
     def tile(level):
         return pl.ds(pl.multiple_of(level * rows, rows), rows)
 
-    def pack(level, packed):
+    def pack(fields, level, packed):
         shift = lax.rem(level + 1, lanes)
-        west, east, flow = packed
         at_e, at_w = lane == level, lane == shift
-        west_new, east_new = [], []
-        for t in range(tracers):
-            turned = pltpu.roll(x[t, tile(level), :], shift, 1)
-            west_new.append(jnp.where(at_w, turned, west[t]))
-            east_new.append(jnp.where(at_e, turned, east[t]))
-        flow = jnp.where(at_e, pltpu.roll(cx[tile(level), :], shift, 1), flow)
-        return tuple(west_new), tuple(east_new), flow
+        packed_new = []
+        for field, (west, east) in zip(fields, packed, strict=True):
+            turned = pltpu.roll(field[tile(level), :], shift, 1)
+            packed_new.append((jnp.where(at_w, turned, west), jnp.where(at_e, turned, east)))
+        return tuple(packed_new)
 
     zero = jnp.zeros((rows, lanes), jnp.float32)
-    west, east, flow = lax.fori_loop(
-        0, levels, pack, ((zero,) * tracers, (zero,) * tracers, zero), unroll=16
-    )
-    for t in range(tracers):
-        pack_w[t] = west[t]
-        pack_e[t] = east[t]
-    pack_e[tracers] = flow
+    loads[0].wait()
+    for t in range(0, tracers, 2):
+        loads[1 + t].wait()
+        loads[2 + t].wait()
+        fields = [x.at[t], x.at[t + 1]] + ([cx] if t == 0 else [])
+        packed = lax.fori_loop(
+            0,
+            levels,
+            functools.partial(pack, fields),
+            ((zero, zero),) * len(fields),
+            unroll=32,
+        )
+        for u, (west, east) in enumerate(packed[:2]):
+            pack_w[t + u] = west
+            pack_e[t + u] = east
+        if t == 0:
+            pack_e[tracers] = packed[2][1]
     go_w = pltpu.make_async_remote_copy(
         src_ref=pack_w, dst_ref=from_e, send_sem=lon_send.at[0], recv_sem=lon_recv.at[0],
         device_id=to_w, device_id_type=MESH,
@@ -245,15 +297,19 @@
         src_ref=pack_e, dst_ref=from_w, send_sem=lon_send.at[1], recv_sem=lon_recv.at[1],
         device_id=to_e, device_id_type=MESH,
     )
+    pl.semaphore_wait(barrier, peers)
     go_w.start()
     go_e.start()
-    for k in range(AHEAD):
-        pass_on(k)
+    for k in range(chunks):
+        send(k, detour)
+    for k in range(chunks):
+        send(k, outgoing)
+    for c in loads[1 + tracers :]:
+        c.wait()
     go_w.wait()
     go_e.wait()
-    for k in range(AHEAD, chunks):
+    for k in range(chunks):
         pass_on(k)
-        send(k, outgoing)
     flow = from_w[tracers]
     for t in range(tracers):
         own = pltpu.roll(pack_w[t], lanes - 1, 1)
@@ -347,11 +403,9 @@
     inner = tuple(range(1, rows - 1))
     lax.fori_loop(0, levels, advect, 0, unroll=4)
     carry = ground(inner)
-    for k in range(chunks):
-        start = levels - 1 - k * CHUNK
-        carry = lax.fori_loop(
-            0, CHUNK, lambda i, c: up(inner, (cp, cq, cd, ca, cs), start - i, c), carry, unroll=4
-        )
+    carry = lax.fori_loop(
+        0, levels, lambda i, c: up(inner, (cp, cq, cd, ca, cs), levels - 1 - i, c), carry, unroll=4
+    )
     sweep(top(inner, carry), (cp, cq, cd, ca, cs), nn)
 
     def total(group, carry):
@@ -367,17 +421,16 @@
     def every(level, row):
         return pl.ds(level * rows + row, 8, stride=rows)
 
-    for k in range(chunks):
-        for here, make in (
-            (has_s, send_cy), (has_s, send_na), (has_s, send_nb), (has_n, send_sa), (has_n, send_sb),
-        ):
+    for k, (low, count) in enumerate(PARTS):
+        for here, make in incoming:
 
             @pl.when(here)
             def _():
                 make(k).wait_recv()
 
-        for level in range(levels - (k + 1) * CHUNK, levels - k * CHUNK, 8):
-            group = pl.ds(level, 8)
+        def edges(i, c):
+            level = low + 8 * i
+            group = pl.ds(pl.multiple_of(level, 8), 8)
             flow_n = jnp.where(last, 0.0, cy[every(level, rows - 1), :])
             flow_s = south[tracers, group, :]
             np_, nm = jnp.maximum(flow_n, 0.0), jnp.minimum(flow_n, 0.0)
@@ -388,9 +441,12 @@
                 at_n, at_s = every(level, rows - 1), every(level, 0)
                 tn[t, at_n, :] = tn[t, at_n, :] - flux_n
                 tn[t, at_s, :] = tn[t, at_s, :] + flux_s
-        start = levels - 1 - k * CHUNK
+            return c
+
+        lax.fori_loop(0, count // 8, edges, 0, unroll=2)
+        start = low + count - 1
         carry = lax.fori_loop(
-            0, CHUNK, lambda i, c: up(outer, (op, oq, od, oa, os), start - i, c), carry, unroll=4
+            0, count, lambda i, c: up(outer, (op, oq, od, oa, os), start - i, c), carry, unroll=4
         )
     for i, (beam, net) in enumerate(top(outer, carry)):
         start_state[pl.ds(2 * i * gs, gs), :] = beam
@@ -403,19 +459,22 @@
             def _():
                 make(k).wait_send()
 
-        @pl.when(first)
-        def _():
-            hop(k, north, SB, to_n).wait_send()
-
-        @pl.when(last)
-        def _():
-            hop(k, south, NB, to_s).wait_send()
+        for at in range(slots):
+
+            @pl.when(first)
+            def _():
+                hop_s(k, at).wait_send()
+
+            @pl.when(last)
+            def _():
+                hop_n(k, at).wait_send()
 
 
 def on_device(tracers, courant_x, courant_y, sunlit, cosine, albedo, absorb, scatter, weight):
     count, levels, rows, lanes = tracers.shape
     gs = absorb.shape[0]
-    chunks = levels // CHUNK
+    chunks = len(PARTS)
+    slots = lax.axis_size("lat") // 2 - 1
     f32 = jnp.float32
     hbm = pl.BlockSpec(memory_space=pltpu.HBM)
     vmem = pl.BlockSpec(memory_space=pltpu.VMEM)
@@ -455,14 +514,15 @@
             pltpu.SMEM((gs,), f32),
             pltpu.VMEM((count, levels, lanes), f32),
             pltpu.VMEM((count + 1, levels, lanes), f32),
-            pltpu.VMEM((count - SHARED, levels, lanes), f32),
+            pltpu.VMEM((slots, 2, levels, lanes), f32),
             pltpu.VMEM((count + 1, rows, lanes), f32),
             pltpu.VMEM((count, rows, lanes), f32),
             pltpu.VMEM((count, rows, lanes), f32),
             pltpu.VMEM((count + 1, rows, lanes), f32),
         ]
         + [inner_layers] * 6
-        + [dma((9,)), dma((chunks, 6)), dma((chunks, 6)), dma((2,)), dma((2,)), dma((chunks,))],
+        + [dma((count + 8,)), dma((chunks, 6)), dma((chunks, 6)), dma((2,)), dma((2,))]
+        + [dma((chunks, slots)), dma((chunks, slots))],
         compiler_params=pltpu.CompilerParams(
             collective_id=0, has_side_effects=True, vmem_limit_bytes=36 * 2**20
         ),

time: 50 us -> 47.3 us (0.946)
  Pallas kernels: 49.3 us -> 46.3 us
    pallas_call x1, Pallas kernels: 47.5 us -> 44.5 us  [on_device(): pl.pallas_call(kernel, out_shape=[pltpu.VMEM((count, flat, lanes), f32),...]
where the time goes in v1:
time: 47.3 us; the launch traced here: 47 us
  Pallas kernels  46.3 us (98%)
  between operations  0.64 us (1%)
    pallas_call x1, Pallas kernels, on_device(): pl.pallas_call(kernel, out_shape=[pltpu.VMEM((count, flat, lanes), f32),...  44.5 us
    pallas_call x1, Pallas kernels, on_device(): pl.pallas_call(finish, out_shape=[pltpu.HBM((count, flat, lanes), f32), p...  1.85 us

profile of v1, /device:TPU:40, one launch (start us, length us, event | category | flops | bytes accessed | tf_op | source)
XLA Modules:
  0.0 47.0 jit_solution(7325990716668318375)
XLA Ops:
  0.6 44.5 %advect_and_heat.1 = (f32[6,1024,128]{2,1,0:T(8,128)S(1)}, f32[1024,128]{1,0:T(8,128)S(1)}, f32[128,16,128]{2,1,0:T(8,128)S(1)}, f32[128,16,128]{2,1,0:T(8,128)S...) custom-call(f32[6,128,8,128]{3,2,1,0:T(8,128)} %x4.1, ...), custom_call_target="tpu_custom_call" | custom-call | tf_op jit(solution)/shard_map/advect_and_heat/pallas_call | solution.py:498
  45.1 1.8 %finish.1 = (f32[6,1024,128]{2,1,0:T(8,128)}, f32[1024,128]{1,0:T(8,128)}) custom-call(f32[6,1024,128]{2,1,0:T(8,128)S(1)} %get-tuple-element.12.tn, f32[1024,128]{1,0:T(8,128)S(1)} %get-tuple-element.13.heat, f32[128,16,128]{2,1,0:T(8,128)S(1)} %get-tuple-element.14.op, f32[128,16,128]{2,1,0:T(8,128)S(1)} %get-tuple-element.15.oq, ...), custom_call_target="tpu_custom_call" | custom-call | tf_op jit(solution)/shard_map/finish/pallas_call | solution.py:531

commit v2 on v1

--- a/solution.py
+++ b/solution.py
@@ -10,7 +10,7 @@
 MESH = pl.DeviceIdType.MESH
 LOG2E = 1.4426950408889634
 PARTS = ((96, 32), (48, 48), (16, 32), (0, 16))
-CY, NA, NB, SA, SB, RELAY = range(6)
+NA, NB, SA, SB, RELAY = range(5)
 
 
 def rcp(value):
@@ -70,10 +70,10 @@
 
 
 def kernel(
-    x4, x3, cx3, cy4, cy3, sunlit_in, cosine_in, albedo_in, absorb_in, scatter_in, weight_in,
+    x4, x3, cx3, cy3, sunlit_in, cosine_in, albedo_in, absorb_in, scatter_in, weight_in,
     tn, heat, op, oq, od, oa, os, start_state,
     x, cx, cy, sunlit, cosine, albedo, absorb, scatter, weight,
-    north, south, relay, pack_e, pack_w, from_e, from_w,
+    rows_n, north, south, relay, pack_e, pack_w, from_e, from_w,
     cp, cq, cd, ca, cs, nn,
     load_sem, send_sem, recv_sem, lon_send, lon_recv, relay_recv, hop_send,
 ):
@@ -147,11 +147,8 @@
     def part(k):
         return pl.ds(*PARTS[k])
 
-    def send_cy(k):
-        return copy(cy4.at[part(k), rows - 1, :], south.at[tracers, part(k)], k, CY, to_n)
-
     def rows_to_n(k, planes, kind):
-        src, dst = x4.at[planes, part(k), rows - 1, :], south.at[planes, part(k)]
+        src, dst = rows_n.at[planes, part(k)], south.at[planes, part(k)]
         return copy(src, dst, k, kind, to_n)
 
     def rows_to_s(k, planes, kind):
@@ -176,9 +173,9 @@
     def send_s(k):
         return rows_to_s(k, pl.ds(0, tracers), SA)
 
-    def detour_row(k, row, at, to):
+    def detour_row(k, planes_of, at, to):
         return pltpu.make_async_remote_copy(
-            src_ref=x4.at[shared(k), part(k), row, :],
+            src_ref=planes_of,
             dst_ref=relay.at[at, pl.ds(0, 1 + k % 2), part(k)],
             send_sem=send_sem.at[k, RELAY],
             recv_sem=relay_recv.at[k, at],
@@ -187,10 +184,10 @@
         )
 
     def send_rs(k):
-        return detour_row(k, 0, slot, 0)
+        return detour_row(k, x4.at[shared(k), part(k), 0, :], slot, 0)
 
     def send_rn(k):
-        return detour_row(k, rows - 1, slot, n_lat - 1)
+        return detour_row(k, rows_n.at[shared(k), part(k)], slot, n_lat - 1)
 
     def hop(k, at, dst, kind, to):
         return pltpu.make_async_remote_copy(
@@ -208,18 +205,18 @@
     def hop_n(k, at):
         return hop(k, at, south, NB, 2 * at + 2)
 
-    detour = [(via_first, send_rs), (via_last, send_rn)]
-    outgoing = [
-        (has_n, send_cy),
+    detour_s, detour_n = [(via_first, send_rs)], [(via_last, send_rn)]
+    northward = [
         (jnp.logical_and(has_n, jnp.logical_not(via_last)), send_n),
         (via_last, send_na),
+    ]
+    southward = [
         (jnp.logical_and(has_s, jnp.logical_not(via_first)), send_s),
         (via_first, send_sa),
     ]
     whole_s, split_s = jnp.logical_and(has_s, jnp.logical_not(even)), jnp.logical_and(has_s, even)
     whole_n, split_n = jnp.logical_and(has_n, even), jnp.logical_and(has_n, jnp.logical_not(even))
     incoming = [
-        (has_s, send_cy),
         (whole_s, send_n),
         (split_s, send_na),
         (split_s, send_nb),
@@ -233,12 +230,12 @@
 
             @pl.when(first)
             def _():
-                detour_row(k, 0, at, 0).wait_recv()
+                detour_row(k, x4.at[shared(k), part(k), 0, :], at, 0).wait_recv()
                 hop_s(k, at).start()
 
             @pl.when(last)
             def _():
-                detour_row(k, rows - 1, at, n_lat - 1).wait_recv()
+                detour_row(k, rows_n.at[shared(k), part(k)], at, n_lat - 1).wait_recv()
                 hop_n(k, at).start()
 
     def send(k, which):
@@ -261,6 +258,9 @@
 
     def tile(level):
         return pl.ds(pl.multiple_of(level * rows, rows), rows)
+
+    def every(level, row):
+        return pl.ds(level * rows + row, 8, stride=rows)
 
     def pack(fields, level, packed):
         shift = lax.rem(level + 1, lanes)
@@ -301,11 +301,27 @@
     go_w.start()
     go_e.start()
     for k in range(chunks):
-        send(k, detour)
-    for k in range(chunks):
-        send(k, outgoing)
+        send(k, detour_s)
+    send(0, southward)
     for c in loads[1 + tracers :]:
         c.wait()
+
+    def gather(group, carry):
+        at = pl.ds(pl.multiple_of(group * 8, 8), 8)
+        flow = cy[every(group * 8, rows - 1), :]
+        inward = jnp.maximum(flow, 0.0)
+        for t in range(tracers):
+            share = inward * x[t, every(group * 8, rows - 1), :]
+            rows_n[t, at, :] = jnp.where(flow < 0.0, flow, share) if t == 0 else share
+        return carry
+
+    lax.fori_loop(0, levels // 8, gather, 0, unroll=4)
+    for k in range(chunks):
+        send(k, detour_n)
+    send(0, northward)
+    for k in range(1, chunks):
+        send(k, southward)
+        send(k, northward)
     go_w.wait()
     go_e.wait()
     for k in range(chunks):
@@ -418,9 +434,6 @@
     outer = (0, rows - 1)
     carry = ground(outer)
 
-    def every(level, row):
-        return pl.ds(level * rows + row, 8, stride=rows)
-
     for k, (low, count) in enumerate(PARTS):
         for here, make in incoming:
 
@@ -432,12 +445,13 @@
             level = low + 8 * i
             group = pl.ds(pl.multiple_of(level, 8), 8)
             flow_n = jnp.where(last, 0.0, cy[every(level, rows - 1), :])
-            flow_s = south[tracers, group, :]
+            flow_s = south[0, group, :]
             np_, nm = jnp.maximum(flow_n, 0.0), jnp.minimum(flow_n, 0.0)
-            sp, sm = jnp.maximum(flow_s, 0.0), jnp.minimum(flow_s, 0.0)
+            sm = jnp.minimum(flow_s, 0.0)
             for t in range(tracers):
                 flux_n = np_ * x[t, every(level, rows - 1), :] + nm * north[t, group, :]
-                flux_s = sp * south[t, group, :] + sm * x[t, every(level, 0), :]
+                share = south[t, group, :] if t else jnp.maximum(flow_s, 0.0)
+                flux_s = share + sm * x[t, every(level, 0), :]
                 at_n, at_s = every(level, rows - 1), every(level, 0)
                 tn[t, at_n, :] = tn[t, at_n, :] - flux_n
                 tn[t, at_s, :] = tn[t, at_s, :] + flux_s
@@ -453,7 +467,7 @@
         start_state[pl.ds((2 * i + 1) * gs, gs), :] = net
 
     for k in range(chunks):
-        for here, make in outgoing + detour:
+        for here, make in northward + southward + detour_n + detour_s:
 
             @pl.when(here)
             def _():
@@ -486,7 +500,6 @@
         tracers,
         tracers.reshape(count, flat, lanes),
         courant_x.reshape(flat, lanes),
-        courant_y,
         courant_y.reshape(flat, lanes),
         sunlit,
         cosine,
@@ -500,7 +513,7 @@
         out_shape=[pltpu.VMEM((count, flat, lanes), f32), pltpu.VMEM((flat, lanes), f32)]
         + [outer_layers] * 5
         + [pltpu.VMEM((4 * gs, lanes), f32)],
-        in_specs=[hbm] * 11,
+        in_specs=[hbm] * 10,
         out_specs=[vmem] * 8,
         scratch_shapes=[
             pltpu.VMEM((count, flat, lanes), f32),
@@ -513,7 +526,8 @@
             pltpu.SMEM((gs,), f32),
             pltpu.SMEM((gs,), f32),
             pltpu.VMEM((count, levels, lanes), f32),
-            pltpu.VMEM((count + 1, levels, lanes), f32),
+            pltpu.VMEM((count, levels, lanes), f32),
+            pltpu.VMEM((count, levels, lanes), f32),
             pltpu.VMEM((slots, 2, levels, lanes), f32),
             pltpu.VMEM((count + 1, rows, lanes), f32),
             pltpu.VMEM((count, rows, lanes), f32),
@@ -521,7 +535,7 @@
             pltpu.VMEM((count + 1, rows, lanes), f32),
         ]
         + [inner_layers] * 6
-        + [dma((count + 8,)), dma((chunks, 6)), dma((chunks, 6)), dma((2,)), dma((2,))]
+        + [dma((count + 8,)), dma((chunks, 5)), dma((chunks, 5)), dma((2,)), dma((2,))]
         + [dma((chunks, slots)), dma((chunks, slots))],
         compiler_params=pltpu.CompilerParams(
             collective_id=0, has_side_effects=True, vmem_limit_bytes=36 * 2**20

time: 47.3 us -> 45.8 us (0.968)
  Pallas kernels: 46.3 us -> 45.1 us
    pallas_call x1, Pallas kernels: 44.5 us -> 43.2 us  [on_device(): pl.pallas_call(kernel, out_shape=[pltpu.VMEM((count, flat, lanes), f32),...]
where the time goes in v2:
time: 45.8 us; the launch traced here: 45.7 us
  Pallas kernels  45.1 us (98%)
  between operations  0.64 us (1%)
    pallas_call x1, Pallas kernels, on_device(): pl.pallas_call(kernel, out_shape=[pltpu.VMEM((count, flat, lanes), f32),...  43.2 us
    pallas_call x1, Pallas kernels, on_device(): pl.pallas_call(finish, out_shape=[pltpu.HBM((count, flat, lanes), f32), p...  1.85 us

profile of v2, /device:TPU:40, one launch (start us, length us, event | category | flops | bytes accessed | tf_op | source)
XLA Modules:
  0.0 45.7 jit_solution(11930744986225900117)
XLA Ops:
  0.6 43.2 %advect_and_heat.1 = (f32[6,1024,128]{2,1,0:T(8,128)S(1)}, f32[1024,128]{1,0:T(8,128)S(1)}, f32[128,16,128]{2,1,0:T(8,128)S(1)}, f32[128,16,128]{2,1,0:T(8,128)S...) custom-call(f32[6,128,8,128]{3,2,1,0:T(8,128)} %x4.1, ...), custom_call_target="tpu_custom_call" | custom-call | tf_op jit(solution)/shard_map/advect_and_heat/pallas_call | solution.py:511
  43.9 1.8 %finish.1 = (f32[6,1024,128]{2,1,0:T(8,128)}, f32[1024,128]{1,0:T(8,128)}) custom-call(f32[6,1024,128]{2,1,0:T(8,128)S(1)} %get-tuple-element.12.tn, f32[1024,128]{1,0:T(8,128)S(1)} %get-tuple-element.13.heat, f32[128,16,128]{2,1,0:T(8,128)S(1)} %get-tuple-element.14.op, f32[128,16,128]{2,1,0:T(8,128)S(1)} %get-tuple-element.15.oq, ...), custom_call_target="tpu_custom_call" | custom-call | tf_op jit(solution)/shard_map/finish/pallas_call | solution.py:545

commit v3 on v2

--- a/solution.py
+++ b/solution.py
@@ -9,7 +9,7 @@
 
 MESH = pl.DeviceIdType.MESH
 LOG2E = 1.4426950408889634
-PARTS = ((96, 32), (48, 48), (16, 32), (0, 16))
+PARTS = ((96, 32), (48, 48), (8, 40), (0, 8))
 NA, NB, SA, SB, RELAY = range(5)
 
 
@@ -282,7 +282,7 @@
             levels,
             functools.partial(pack, fields),
             ((zero, zero),) * len(fields),
-            unroll=32,
+            unroll=levels,
         )
         for u, (west, east) in enumerate(packed[:2]):
             pack_w[t + u] = west

time: 45.8 us -> 45 us (0.983)
  Pallas kernels: 45.1 us -> 44.2 us
    pallas_call x1, Pallas kernels: 43.2 us -> 42.3 us  [on_device(): pl.pallas_call(kernel, out_shape=[pltpu.VMEM((count, flat, lanes), f32),...]
where the time goes in v3:
time: 45 us; the launch traced here: 44.8 us
  Pallas kernels  44.2 us (98%)
  between operations  0.64 us (1%)
    pallas_call x1, Pallas kernels, on_device(): pl.pallas_call(kernel, out_shape=[pltpu.VMEM((count, flat, lanes), f32),...  42.3 us
    pallas_call x1, Pallas kernels, on_device(): pl.pallas_call(finish, out_shape=[pltpu.HBM((count, flat, lanes), f32), p...  1.85 us

profile of v3, /device:TPU:40, one launch (start us, length us, event | category | flops | bytes accessed | tf_op | source)
XLA Modules:
  0.0 44.8 jit_solution(14108817851437574238)
XLA Ops:
  0.6 42.3 %advect_and_heat.1 = (f32[6,1024,128]{2,1,0:T(8,128)S(1)}, f32[1024,128]{1,0:T(8,128)S(1)}, f32[128,16,128]{2,1,0:T(8,128)S(1)}, f32[128,16,128]{2,1,0:T(8,128)S...) custom-call(f32[6,128,8,128]{3,2,1,0:T(8,128)} %x4.1, ...), custom_call_target="tpu_custom_call" | custom-call | tf_op jit(solution)/shard_map/advect_and_heat/pallas_call | solution.py:511
  43.0 1.8 %finish.1 = (f32[6,1024,128]{2,1,0:T(8,128)}, f32[1024,128]{1,0:T(8,128)}) custom-call(f32[6,1024,128]{2,1,0:T(8,128)S(1)} %get-tuple-element.12.tn, f32[1024,128]{1,0:T(8,128)S(1)} %get-tuple-element.13.heat, f32[128,16,128]{2,1,0:T(8,128)S(1)} %get-tuple-element.14.op, f32[128,16,128]{2,1,0:T(8,128)S(1)} %get-tuple-element.15.oq, ...), custom_call_target="tpu_custom_call" | custom-call | tf_op jit(solution)/shard_map/finish/pallas_call | solution.py:545

commit v4 on v3

--- a/solution.py
+++ b/solution.py
@@ -9,7 +9,7 @@
 
 MESH = pl.DeviceIdType.MESH
 LOG2E = 1.4426950408889634
-PARTS = ((96, 32), (48, 48), (8, 40), (0, 8))
+PARTS = ((72, 56), (8, 64), (0, 8))
 NA, NB, SA, SB, RELAY = range(5)
 
 

time: 45 us -> 44.8 us (level)
  no operation moved by 1% of the time
where the time goes in v4:
time: 44.8 us; the launch traced here: 44.7 us
  Pallas kernels  44.1 us (98%)
  between operations  0.64 us (1%)
    pallas_call x1, Pallas kernels, on_device(): pl.pallas_call(kernel, out_shape=[pltpu.VMEM((count, flat, lanes), f32),...  42.2 us
    pallas_call x1, Pallas kernels, on_device(): pl.pallas_call(finish, out_shape=[pltpu.HBM((count, flat, lanes), f32), p...  1.85 us

profile of v4, /device:TPU:40, one launch (start us, length us, event | category | flops | bytes accessed | tf_op | source)
XLA Modules:
  0.0 44.7 jit_solution(4943279994660169083)
XLA Ops:
  0.6 42.2 %advect_and_heat.1 = (f32[6,1024,128]{2,1,0:T(8,128)S(1)}, f32[1024,128]{1,0:T(8,128)S(1)}, f32[128,16,128]{2,1,0:T(8,128)S(1)}, f32[128,16,128]{2,1,0:T(8,128)S...) custom-call(f32[6,128,8,128]{3,2,1,0:T(8,128)} %x4.1, ...), custom_call_target="tpu_custom_call" | custom-call | tf_op jit(solution)/shard_map/advect_and_heat/pallas_call | solution.py:511
  42.9 1.8 %finish.1 = (f32[6,1024,128]{2,1,0:T(8,128)}, f32[1024,128]{1,0:T(8,128)}) custom-call(f32[6,1024,128]{2,1,0:T(8,128)S(1)} %get-tuple-element.12.tn, f32[1024,128]{1,0:T(8,128)S(1)} %get-tuple-element.13.heat, f32[128,16,128]{2,1,0:T(8,128)S(1)} %get-tuple-element.14.op, f32[128,16,128]{2,1,0:T(8,128)S(1)} %get-tuple-element.15.oq, ...), custom_call_target="tpu_custom_call" | custom-call | tf_op jit(solution)/shard_map/finish/pallas_call | solution.py:545
